TPU v7x, 32 devices: a whole 2x2x4 slice. The times are simulated.
32 devices in a mesh: rep: 2 (over x), node: 16 (over z, y, core).
Axes of the slice: x: 2, y: 2, z: 4, core: 2. Of those that a mesh axis runs over, the one named last changes fastest.
Arguments:
- tokens: bfloat16 [4096, 7168], P(('rep', 'node')), parts along dimension 0, may hold values from -6 to 6
- group_choice: int32 [4096, 4], P(('rep', 'node')), parts along dimension 0, may hold values from 0 to 7, as said below
- expert_picks: int32 [4096, 8], P(('rep', 'node')), parts along dimension 0, may hold values from 0 to 255, as said below
- gate_fixed: int32 [4096, 8], P(('rep', 'node')), parts along dimension 0, may hold values from 1 to 65535
- token_counts: int32 [32], P(('rep', 'node')), parts along dimension 0, may hold values from 16 to 128, as said below
- expert_gate: bfloat16 [7168, 2048], P(None, 'node'), may hold values from -0.0625 to 0.0625
- expert_up: bfloat16 [7168, 2048], P(None, 'node'), may hold values from -0.0625 to 0.0625
- expert_down: bfloat16 [2048, 7168], P('node'), may hold values from -0.1875 to 0.1875
Outputs:
- routed_out: bfloat16 [4096, 7168], P(('rep', 'node')), parts along dimension 0
There are 2 independent parts, one for each index of `rep`. A program takes and returns all parts, laid end to end along the dimension named above; an argument that names none is the same for every part. Nothing has to cross between parts.
Inputs may be any that keep to these rules, and one draw needn't show every extreme that they name: `group_choice`: each row holds 4 different groups. `expert_picks`: each row names 8 different experts, two from each group of the same row of group_choice (expert e lies in group e // 32); at most one of them is a held expert f * 32 with f < 2. Among the valid tokens of one device each held expert is picked at most 8 times, and in every draw one held expert is picked exactly 8 times on every device. `token_counts`: some device has 128 valid tokens and some device 2 * 8.
All inputs are finite; a program needn't handle non-finite values.
Results may differ from a plain program's by a relative error of at most 0.0064.
Values may be sent and summed in bfloat16 or wider, within the bound.
A program may use at most 64 MiB of HBM per device.

v0:
```python
import jax
import jax.numpy as jnp
from jax import lax
from jax.sharding import PartitionSpec as P

SPLIT = 8
GROUP_SIZE = 32


def expert_partial(rows_in, expert_gate, expert_up, expert_down):
    shape_in = rows_in.shape
    flat_rows = rows_in.reshape(-1, shape_in[-1])
    gate_val = jnp.dot(flat_rows, expert_gate, preferred_element_type=jnp.float32)
    up_val = jnp.dot(flat_rows, expert_up, preferred_element_type=jnp.float32)
    hidden = (jax.nn.silu(gate_val) * up_val).astype(jnp.bfloat16)
    partial_out = jnp.dot(hidden, expert_down, preferred_element_type=jnp.float32).astype(
        jnp.bfloat16
    )
    return partial_out.reshape(shape_in[:-1] + (expert_down.shape[1],))


def local(
    tokens,
    group_choice,
    expert_picks,
    gate_fixed,
    token_counts,
    expert_gate,
    expert_up,
    expert_down,
):
    devices = lax.axis_size("node")
    flight = devices // SPLIT
    row_count = tokens.shape[0]
    capacity = row_count // 16
    positions = jnp.arange(row_count, dtype=jnp.int32)
    is_valid = positions < token_counts[0]
    gate_vals = gate_fixed.astype(jnp.float32)
    weight = 2.5 * gate_vals / jnp.sum(gate_vals, axis=1, keepdims=True)
    in_group = jnp.any((expert_picks // GROUP_SIZE)[:, :, None] == group_choice[:, None, :], axis=2)
    counted = in_group & is_valid[:, None]
    targets = jnp.arange(flight, dtype=jnp.int32) * GROUP_SIZE
    matches = counted[:, :, None] & (expert_picks[:, :, None] == targets[None, None, :])
    picked = jnp.any(matches, axis=1)
    shares = jnp.sum(jnp.where(matches, weight[:, :, None], 0.0), axis=1)
    slot_of = jnp.cumsum(picked.astype(jnp.int32), axis=0) - 1
    slot_ids = jnp.arange(capacity, dtype=jnp.int32)
    slot_hit = picked.T[:, None, :] & (slot_of.T[:, None, :] == slot_ids[None, :, None])
    source_row = jnp.sum(jnp.where(slot_hit, positions[None, None, :], 0), axis=2)
    slot_used = jnp.any(slot_hit, axis=2)
    outgoing = jnp.where(
        slot_used[:, :, None], jnp.take(tokens, source_row, axis=0), jnp.zeros((), jnp.bfloat16)
    )
    copies = jnp.repeat(outgoing, SPLIT, axis=0)
    returned = lax.all_to_all(
        expert_partial(
            lax.all_to_all(copies, "node", split_axis=0, concat_axis=0, tiled=True),
            expert_gate,
            expert_up,
            expert_down,
        ),
        "node",
        split_axis=0,
        concat_axis=0,
        tiled=True,
    )
    summed = jnp.sum(
        returned.reshape((flight, SPLIT) + returned.shape[1:]), axis=1, dtype=jnp.float32
    )
    expert_out = summed.astype(jnp.bfloat16)
    result = jnp.zeros((row_count, tokens.shape[1]), jnp.float32)
    for expert in range(flight):
        rows_back = jnp.take(
            expert_out[expert], jnp.clip(slot_of[:, expert], 0, capacity - 1), axis=0
        )
        result = result + shares[:, expert : expert + 1] * rows_back.astype(jnp.float32)
    return result.astype(jnp.bfloat16)


def solution(mesh):
    return jax.shard_map(
        local,
        mesh=mesh,
        in_specs=(
            P(("rep", "node"), None),
            P(("rep", "node"), None),
            P(("rep", "node"), None),
            P(("rep", "node"), None),
            P(("rep", "node")),
            P(None, "node"),
            P(None, "node"),
            P("node", None),
        ),
        out_specs=P(("rep", "node"), None),
        check_vma=False,
    )
```

profile of v0, /device:TPU:15, one launch (start us, length us, event | category | flops | bytes accessed | tf_op | source)
XLA Modules:
  0.0 121.0 jit_solution(17459301770604360620)
XLA Ops:
  0.0 0.0 copy-start
  0.8 0.7 add_select_fusion
  1.5 0.7 compare_reduce_fusion
  2.2 0.8 fusion.24
  3.0 0.1 copy.21
  3.1 0.2 reduce_window_sum.11
  3.3 0.1 copy.22
  3.3 0.2 fusion.23
  3.5 0.2 select_reduce_fusion
  3.7 0.1 reshape.96
  3.8 2.6 %gather_fusion = bf16[16,7168]{1,0:T(8,128)(2,1)S(1)} fusion(bf16[128,7168]{1,0:T(8,128)(2,1)} %param.10, s32[1024]{0:T(1024)S(1)} %pad_clamp_fusion.2), kind=kCustom, calls=%fused_computation.2 | custom fusion | bytes 458816 | tf_op jit(solution)/shard_map/jit(_take)/gather | solution.py:52
  6.4 0.1 fusion.13
  6.5 0.2 broadcast_in_dim.79
  6.7 0.0 copy-start.2
  6.7 48.2 %all_to_all.10 = bf16[16,8,7168]{2,1,0:T(8,128)(2,1)S(1)} all-to-all(bf16[16,8,7168]{2,1,0:T(8,128)(2,1)S(1)} %bitcast.40), channel_id=1, replica_groups=mesh['rep'=2,'node'=16] {'node'}, dimensions={0} | all-to-all | bytes 3670016 | tf_op jit(solution)/shard_map/all_to_all | solution.py:57
  54.9 0.0 copy-start.1
  54.9 1.2 %copy-done.1 = bf16[16,8,7168]{2,1,0:T(8,128)(2,1)} copy-done((bf16[16,8,7168]{2,1,0:T(8,128)(2,1)}, bf16[16,8,7168]{2,1,0:T(8,128)(2,1)S(1)}, u32[]{:S(2)}) %copy-start.1) | copy-done | bytes 1835032
  56.1 0.0 copy-done.2
  56.1 0.6 fusion.3
  56.7 0.0 copy-done
  56.8 4.5 %fusion = bf16[16,8,7168]{2,1,0:T(8,128)(2,1)} fusion(bf16[128,7168]{1,0:T(8,128)(2,1)S(1)} %copy-done, bf16[7168,128]{1,0:T(8,128)(2,1)} %param.16, bf16[16,8,7168]{2,1,0:T(8,128)(2,1)} %copy-done.1, f32[128,128]{1,0:T(8,128)S(1)} %fusion.3), kind=kOutput, calls=%fused_computation.4 | convolution fusion | flops 470777856 | bytes 7405568 | tf_op jit(solution)/shard_map/dot_general | solution.py:16
  61.3 0.0 copy-start.4
  61.3 0.0 copy-start.3
  61.3 5.5 %all-to-all-start.1 = ((bf16[16,8,7168]{2,1,0:T(8,128)(2,1)}), bf16[16,8,7168]{2,1,0:T(8,128)(2,1)}, u32[]{:S(2)}, u32[]{:S(2)}) async-start(bf16[16,8,7168]{2,1,0:T(8,128)(2,1)} %fusion), calls=%async_computation.1 | async-start | bytes 3670016 | tf_op jit(solution)/shard_map/all_to_all | solution.py:55
  66.7 0.2 fusion.15
  67.0 0.0 copy-done.4
  67.0 0.0 copy-done.3
  67.0 0.1 select_reduce_fusion.1
  67.1 41.5 %all-to-all-done.1 = bf16[16,8,7168]{2,1,0:T(8,128)(2,1)} async-done(((bf16[16,8,7168]{2,1,0:T(8,128)(2,1)}), bf16[16,8,7168]{2,1,0:T(8,128)(2,1)}, u32[]{:S(2)}, u32[]{:S(2)}) %all-to-all-start.1) | async-done | bytes 1835040 | tf_op jit(solution)/shard_map/all_to_all | solution.py:55
  108.7 1.7 %bitcast_reduce_fusion = bf16[2,8,7168]{2,1,0:T(8,128)(2,1)S(1)} fusion(bf16[16,8,7168]{2,1,0:T(8,128)(2,1)} %all-to-all-done.1), kind=kLoop, calls=%fused_computation.6 | loop fusion | flops 802816 | bytes 2064384 | tf_op jit(solution)/shard_map/reduce_sum | solution.py:67
  110.4 3.0 %gather_fusion.1 = bf16[128,7168]{1,0:T(8,128)(2,1)} fusion(bf16[8,7168]{1,0:T(8,128)(2,1)S(1)} %get-tuple-element.8, s32[1024]{0:T(1024)S(1)} %pad_clamp_fusion.1), kind=kCustom, calls=%fused_computation.clone | custom fusion | bytes 3670528 | tf_op jit(solution)/shard_map/jit(_take)/gather | solution.py:73
  113.4 2.9 %gather_fusion.2 = bf16[128,7168]{1,0:T(8,128)(2,1)} fusion(bf16[8,7168]{1,0:T(8,128)(2,1)S(1)} %get-tuple-element.9, s32[1024]{0:T(1024)S(1)} %pad_clamp_fusion), kind=kCustom, calls=%fused_computation.1.clone | custom fusion | bytes 3670528 | tf_op jit(solution)/shard_map/jit(_take)/gather | solution.py:73
  116.3 4.7 %add_convert_fusion = bf16[128,7168]{1,0:T(8,128)(2,1)} fusion(bf16[128,7168]{1,0:T(8,128)(2,1)} %gather_fusion.2, bf16[128,7168]{1,0:T(8,128)(2,1)} %gather_fusion.1, f32[128]{0:T(128)S(1)} %get-tuple-element.13, f32[128]{0:T(128)S(1)} %get-tuple-element.12, pred[128]{0:T(512)(128)(4,1)S(1)} %get-tuple-element.16, pred[128]{0:T(512)(128)(4,1)S(1)} %get-tuple-element.17), kind=kLoop, calls=%fused_computation.5 | loop fusion | flops 7340032 | bytes 5506304 | tf_op jit(solution)/shard_map/convert_element_type | solution.py:77
  (16 shorter events, 0.1 us)
Async XLA Ops:
  0.0 56.7 %copy-start = (bf16[128,7168]{1,0:T(8,128)(2,1)S(1)}, bf16[128,7168]{1,0:T(8,128)(2,1)}, u32[]{:S(2)}) copy-start(bf16[128,7168]{1,0:T(8,128)(2,1)} %param.17) | copy-start | bytes 5505028
  6.7 49.4 %copy-start.2 = (bf16[7168,128]{1,0:T(8,128)(2,1)S(1)}, bf16[7168,128]{1,0:T(8,128)(2,1)}, u32[]{:S(2)}) copy-start(bf16[7168,128]{1,0:T(8,128)(2,1)} %param.15) | copy-start | bytes 5505028
  54.9 1.2 %copy-start.1 = (bf16[16,8,7168]{2,1,0:T(8,128)(2,1)}, bf16[16,8,7168]{2,1,0:T(8,128)(2,1)S(1)}, u32[]{:S(2)}) copy-start(bf16[16,8,7168]{2,1,0:T(8,128)(2,1)S(1)} %all_to_all.10) | copy-start | bytes 5505028
  61.3 5.7 %copy-start.4 = (s32[128,8]{0,1:T(8,128)S(1)}, s32[128,8]{0,1:T(8,128)}, u32[]{:S(2)}) copy-start(s32[128,8]{0,1:T(8,128)} %param.13) | copy-start | bytes 12292
  61.3 5.7 %copy-start.3 = (s32[128,8]{0,1:T(8,128)S(1)}, s32[128,8]{0,1:T(8,128)}, u32[]{:S(2)}) copy-start(s32[128,8]{0,1:T(8,128)} %param.12) | copy-start | bytes 12292
  61.3 47.4 %all-to-all-start.1 = ((bf16[16,8,7168]{2,1,0:T(8,128)(2,1)}), bf16[16,8,7168]{2,1,0:T(8,128)(2,1)}, u32[]{:S(2)}, u32[]{:S(2)}) async-start(bf16[16,8,7168]{2,1,0:T(8,128)(2,1)} %fusion), calls=%async_computation.1 | async-start | bytes 3670016 | tf_op jit(solution)/shard_map/all_to_all | solution.py:55
where the time goes:
time: 121 us
  blocking collectives  48.2 us (40%)
  waiting for transfers between devices  41.5 us (34%)
  local copies, waits for them, and re-layouts  10.2 us (8%)
  other arithmetic  9.53 us (8%)
  starting transfers between devices  5.48 us (5%)
  matrix products  5.12 us (4%)
    all_to_all x1, blocking collectives, local(): lax.all_to_all(copies, 'node', split_axis=0, concat_axis=0, tiled=True)  48.2 us
    all_to_all x1, waiting for transfers between devices, local(): lax.all_to_all(expert_partial(lax.all_to_all(copies, 'node', split_axis=0...  41.5 us
    gather x2, local copies, waits for them, and re-layouts, local(): jnp.take(expert_out[expert], jnp.clip(slot_of[:, expert], 0, capacity - 1...  5.89 us
    all_to_all x1, starting transfers between devices, local(): lax.all_to_all(expert_partial(lax.all_to_all(copies, 'node', split_axis=0...  5.48 us
    convert_element_type x1, other arithmetic, local(): return result.astype(jnp.bfloat16)  4.66 us
    dot_general x1, matrix products, expert_partial(): jnp.dot(hidden, expert_down, preferred_element_type=jnp.float32)  4.49 us
    gather x1, local copies, waits for them, and re-layouts, local(): jnp.take(tokens, source_row, axis=0)  2.63 us
  transfers between devices with their start and end apart: 1, of which 1 were waited for; matrix products, arithmetic and copies ran while one was open for 0% of the time, Pallas kernels for 0%

commit v1 on v0

v1 whole, which is shorter than its diff:
```python
import functools

import jax
import jax.numpy as jnp
from jax import lax
from jax.experimental import pallas as pl
from jax.experimental.pallas import tpu as pltpu
from jax.sharding import PartitionSpec as P

SPLIT = 8
GROUP_SIZE = 32
MESH = pl.DeviceIdType.MESH
SIB, NEAR, FAR = 1, 2, 4


def kernel(
    flight,
    cap,
    tokens_hbm,
    groups_ref,
    picks_ref,
    gates_ref,
    count_ref,
    gate_hbm,
    up_hbm,
    down_hbm,
    hit_ref,
    share_ref,
    outs_ref,
    tok,
    wgate,
    wup,
    wdown,
    send_unit,
    rows,
    part,
    part_bf,
    diag_in,
    sums_in,
    home_out,
    home_in,
    tok_sem,
    own_sem,
    wsend_sem,
    wrecv_sem,
    usend_sem,
    urecv_sem,
    nsend_sem,
    fsend_sem,
    rrecv_sem,
    dsend_sem,
    drecv_sem,
    ssend_sem,
    srecv_sem,
    hsend_sem,
    hrecv_sem,
):
    me = lax.axis_index("node")
    core = lax.rem(me, 2)
    group = me // SPLIT
    member = lax.rem(me, SPLIT)
    width = tok.shape[1]
    hid = gate_hbm.shape[1]
    token_rows = tok.shape[0]

    def flipped(bit):
        return me + bit - 2 * bit * lax.rem(me // bit, 2)

    sib, near, far = flipped(SIB), flipped(NEAR), flipped(FAR)

    def peer(step):
        return lax.rem(group + step, flight) * SPLIT + member

    tok_copy = pltpu.make_async_copy(tokens_hbm, tok, tok_sem)
    tok_copy.start()

    barrier = pltpu.get_barrier_semaphore()
    partners = [sib, near, far] + [peer(step) for step in range(1, flight)]
    for partner in partners:
        pl.semaphore_signal(barrier, inc=1, device_id={"node": partner}, device_id_type=MESH)

    mine, theirs = pl.ds(0, hid), pl.ds(hid, hid)
    own_copies = [
        pltpu.make_async_copy(gate_hbm, wgate.at[:, mine], own_sem.at[0]),
        pltpu.make_async_copy(up_hbm, wup.at[:, mine], own_sem.at[1]),
        pltpu.make_async_copy(down_hbm, wdown.at[mine, :], own_sem.at[2]),
    ]
    for copy in own_copies:
        copy.start()

    valid = lax.broadcasted_iota(jnp.int32, (token_rows, 1), 0) < count_ref[0]
    gate_vals = gates_ref[...].astype(jnp.float32)
    weight = 2.5 * gate_vals / jnp.sum(gate_vals, axis=1, keepdims=True)
    picks = picks_ref[...]
    groups = groups_ref[...]
    lane = lax.broadcasted_iota(jnp.int32, (token_rows, flight * cap), 1)
    picked = jnp.zeros((token_rows, flight * cap), jnp.float32)
    share = jnp.zeros((token_rows, 1), jnp.float32)
    for step in range(flight):
        expert = lax.rem(group + step, flight)
        chosen = jnp.max((groups == expert).astype(jnp.float32), axis=1, keepdims=True)
        chosen = jnp.where(valid, chosen, 0.0)
        match = (picks == expert * GROUP_SIZE).astype(jnp.float32) * chosen
        share = share + jnp.sum(match * weight, axis=1, keepdims=True)
        here = jnp.max(match, axis=1, keepdims=True)
        in_step = (lane >= step * cap) & (lane < (step + 1) * cap)
        picked = jnp.where(in_step, here, picked)
    below = lax.broadcasted_iota(jnp.int32, (token_rows, token_rows), 0)
    above = lax.broadcasted_iota(jnp.int32, (token_rows, token_rows), 1)
    tri = (above <= below).astype(jnp.bfloat16)
    slot = jnp.dot(tri, picked.astype(jnp.bfloat16), preferred_element_type=jnp.float32) - 1.0
    want = lax.rem(lane, cap).astype(jnp.float32)
    hit = jnp.where(slot == want, picked, 0.0).astype(jnp.bfloat16)
    hit_ref[...] = hit
    share_ref[...] = share

    tok_copy.wait()
    chunk = width // 7 if width % (7 * 128) == 0 else width
    for at in range(0, width, chunk):
        cols = pl.ds(at, chunk)
        got = lax.dot_general(
            hit, tok[:, cols], (((0,), (0,)), ((), ())), preferred_element_type=jnp.float32
        ).astype(jnp.bfloat16)
        for step in range(flight):
            unit = got[step * cap : (step + 1) * cap]
            if step == 0:
                rows[0, 0, :, cols] = unit
            else:
                send_unit[step, :, cols] = unit

    pl.semaphore_wait(barrier, len(partners))

    def remote(src, dst, send_sem, recv_sem, target):
        copy = pltpu.make_async_remote_copy(
            src_ref=src,
            dst_ref=dst,
            send_sem=send_sem,
            recv_sem=recv_sem,
            device_id={"node": target},
            device_id_type=MESH,
        )
        copy.start()
        return copy

    unit_copies = [None]
    for step in range(1, flight):
        unit_copies.append(
            remote(
                send_unit.at[step],
                rows.at[flight - step, 0],
                usend_sem.at[step],
                urecv_sem.at[flight - step],
                peer(step),
            )
        )

    def spread(e):
        return [
            remote(rows.at[e, 0], rows.at[e, 1], nsend_sem.at[e, 0], rrecv_sem.at[e, 0], near),
            remote(rows.at[e, 0], rows.at[e, 2], nsend_sem.at[e, 1], rrecv_sem.at[e, 1], far),
        ]

    via = jnp.where(core == 0, near, far)
    other_via = jnp.where(core == 0, far, near)

    def arrived(dst, recv_sem):
        pltpu.make_async_copy(dst, dst, recv_sem).wait()

    def forward(e):
        src = 2 - core
        arrived(rows.at[e, src], rrecv_sem.at[e, src - 1])
        return remote(rows.at[e, src], rows.at[e, 3], fsend_sem.at[e], rrecv_sem.at[e, 2], via)

    spreads = [spread(0)]
    w_copies = [
        remote(gate_hbm, wgate.at[:, theirs], wsend_sem.at[0], wrecv_sem.at[0], sib),
        remote(up_hbm, wup.at[:, theirs], wsend_sem.at[1], wrecv_sem.at[1], sib),
        remote(down_hbm, wdown.at[theirs, :], wsend_sem.at[2], wrecv_sem.at[2], sib),
    ]
    forwards = [forward(0)]
    for e in range(1, flight):
        arrived(rows.at[e, 0], urecv_sem.at[e])
        spreads.append(spread(e))

    def rest(e):
        arrived(rows.at[e, 1 + core], rrecv_sem.at[e, core])
        arrived(rows.at[e, 3], rrecv_sem.at[e, 2])

    def hidden(low, high):
        count = (high - low) * 4 * cap
        x = rows[low:high].reshape(count, width)
        gate_val = jnp.dot(x, wgate[...], preferred_element_type=jnp.float32)
        up_val = jnp.dot(x, wup[...], preferred_element_type=jnp.float32)
        return (gate_val / (1.0 + jnp.exp(-gate_val)) * up_val).astype(jnp.bfloat16)

    def project(h, low, high):
        for at in range(0, width, chunk):
            cols = pl.ds(at, chunk)
            val = jnp.dot(h, wdown[:, cols], preferred_element_type=jnp.float32)
            val = val.reshape(high - low, 4, cap, chunk)
            part[low:high, :, :, cols] = val
            part_bf[low:high, :, :, cols] = val.astype(jnp.bfloat16)

    def send_diag(e):
        return remote(part_bf.at[e, 3], diag_in.at[e], dsend_sem.at[e], drecv_sem.at[e], other_via)

    rest(0)
    for number in range(2):
        own_copies[number].wait()
        w_copies[number].wait_recv()
    hidden_first = hidden(0, 1)
    for e in range(1, flight):
        forwards.append(forward(e))
    own_copies[2].wait()
    w_copies[2].wait_recv()
    project(hidden_first, 0, 1)
    diags = [send_diag(0)]
    if flight > 1:
        for e in range(1, flight):
            rest(e)
        project(hidden(1, flight), 1, flight)
        for e in range(1, flight):
            diags.append(send_diag(e))

    late = []
    for e in range(flight):
        arrived(diag_in.at[e], drecv_sem.at[e])
        slot_to = 1 + core
        part_bf[e, slot_to] = (part[e, slot_to] + diag_in[e].astype(jnp.float32)).astype(jnp.bfloat16)
        late.append(remote(part_bf.at[e, 1], sums_in.at[e, 0], ssend_sem.at[e, 0], srecv_sem.at[e, 0], near))
        late.append(remote(part_bf.at[e, 2], sums_in.at[e, 1], ssend_sem.at[e, 1], srecv_sem.at[e, 1], far))

    def total(e):
        for way in range(2):
            arrived(sums_in.at[e, way], srecv_sem.at[e, way])
        val = part[e, 0] + sums_in[e, 0].astype(jnp.float32) + sums_in[e, 1].astype(jnp.float32)
        return val.astype(jnp.bfloat16)

    for e in range(1, flight):
        home_out[e] = total(e)
        late.append(
            remote(home_out.at[e], home_in.at[flight - e], hsend_sem.at[e], hrecv_sem.at[flight - e], peer(e))
        )
    outs_ref[0] = total(0)
    for step in range(1, flight):
        arrived(home_in.at[step], hrecv_sem.at[step])
        outs_ref[step] = home_in[step]

    for copy in (
        [c for c in unit_copies if c is not None]
        + [c for pair in spreads for c in pair]
        + forwards
        + w_copies
        + diags
        + late
    ):
        copy.wait_send()


def local(
    tokens,
    group_choice,
    expert_picks,
    gate_fixed,
    token_counts,
    expert_gate,
    expert_up,
    expert_down,
):
    flight = lax.axis_size("node") // SPLIT
    token_rows, width = tokens.shape
    cap = token_rows // 16
    hid = expert_gate.shape[1]
    vmem = pl.BlockSpec(memory_space=pltpu.VMEM)
    anywhere = pl.BlockSpec(memory_space=pl.ANY)
    dma = pltpu.SemaphoreType.DMA
    hit, share, outs = pl.pallas_call(
        functools.partial(kernel, flight, cap),
        out_shape=(
            jax.ShapeDtypeStruct((token_rows, flight * cap), jnp.bfloat16),
            jax.ShapeDtypeStruct((token_rows, 1), jnp.float32),
            jax.ShapeDtypeStruct((flight, cap, width), jnp.bfloat16),
        ),
        in_specs=[
            anywhere,
            vmem,
            vmem,
            vmem,
            pl.BlockSpec(memory_space=pltpu.SMEM),
            anywhere,
            anywhere,
            anywhere,
        ],
        out_specs=(vmem, vmem, vmem),
        scratch_shapes=[
            pltpu.VMEM((token_rows, width), jnp.bfloat16),
            pltpu.VMEM((width, 2 * hid), jnp.bfloat16),
            pltpu.VMEM((width, 2 * hid), jnp.bfloat16),
            pltpu.VMEM((2 * hid, width), jnp.bfloat16),
            pltpu.VMEM((flight, cap, width), jnp.bfloat16),
            pltpu.VMEM((flight, 4, cap, width), jnp.bfloat16),
            pltpu.VMEM((flight, 4, cap, width), jnp.float32),
            pltpu.VMEM((flight, 4, cap, width), jnp.bfloat16),
            pltpu.VMEM((flight, cap, width), jnp.bfloat16),
            pltpu.VMEM((flight, 2, cap, width), jnp.bfloat16),
            pltpu.VMEM((flight, cap, width), jnp.bfloat16),
            pltpu.VMEM((flight, cap, width), jnp.bfloat16),
            dma(()),
            dma((3,)),
            dma((3,)),
            dma((3,)),
            dma((flight,)),
            dma((flight,)),
            dma((flight, 2)),
            dma((flight,)),
            dma((flight, 3)),
            dma((flight,)),
            dma((flight,)),
            dma((flight, 2)),
            dma((flight, 2)),
            dma((flight,)),
            dma((flight,)),
        ],
        compiler_params=pltpu.CompilerParams(
            collective_id=0, has_side_effects=True, vmem_limit_bytes=56 * 1024 * 1024
        ),
    )(tokens, group_choice, expert_picks, gate_fixed, token_counts, expert_gate, expert_up, expert_down)
    back = jnp.dot(hit, outs.reshape(flight * cap, width), preferred_element_type=jnp.float32)
    return (back * share).astype(jnp.bfloat16)


def solution(mesh):
    return jax.shard_map(
        local,
        mesh=mesh,
        in_specs=(
            P(("rep", "node"), None),
            P(("rep", "node"), None),
            P(("rep", "node"), None),
            P(("rep", "node"), None),
            P(("rep", "node")),
            P(None, "node"),
            P(None, "node"),
            P("node", None),
        ),
        out_specs=P(("rep", "node"), None),
        check_vma=False,
    )
```

time: 121 us -> 47.1 us (0.39)
  the two profiles are of different devices: /device:TPU:15 before, /device:TPU:0 now
where the time goes in v1:
time: 47.1 us; the launch traced here: 46.5 us
  Pallas kernels  37.8 us (80%)
  local copies, waits for them, and re-layouts  4.24 us (9%)
  matrix products  2.81 us (6%)
  other arithmetic  0.94 us (2%)
  between operations  0.67 us (1%)
    pallas_call x1, Pallas kernels, local(): pl.pallas_call(functools.partial(kernel, flight, cap), out_shape=(jax.Sha...  37.8 us
    unnamed x3, local copies, waits for them, and re-layouts  4.24 us
    dot_general x1, matrix products, local(): jnp.dot(hit, outs.reshape(flight * cap, width), preferred_element_type=jn...  2.81 us
    pallas_call x1, other arithmetic, local(): pl.pallas_call(functools.partial(kernel, flight, cap), out_shape=(jax.Sha...  0.94 us

profile of v1, /device:TPU:0, one launch (start us, length us, event | category | flops | bytes accessed | tf_op | source)
XLA Modules:
  0.0 46.5 jit_solution(14163188833226929306)
XLA Ops:
  0.7 1.4 %copy.12.groups_ref = s32[128,4]{1,0:T(8,128)} copy(s32[128,4]{0,1:T(4,128)} %param.9) | data formatting | bytes 4096 | tf_op args[1]
  2.1 1.4 %copy.13.picks_ref = s32[128,8]{1,0:T(8,128)} copy(s32[128,8]{0,1:T(8,128)} %param.10) | data formatting | bytes 8192 | tf_op args[2]
  3.5 1.4 %copy.14.gates_ref = s32[128,8]{1,0:T(8,128)} copy(s32[128,8]{0,1:T(8,128)} %param.11) | data formatting | bytes 8192 | tf_op args[3]
  4.9 37.8 %shard_map.82 = (bf16[128,16]{1,0:T(8,128)(2,1)}, f32[128,1]{1,0:T(8,128)}, bf16[2,8,7168]{2,1,0:T(8,128)(2,1)}) custom-call(bf16[128,7168]{1,0:T(8,128)(2,1)} %tokens_hbm.1, s32[128,4]{1,0:T(8,128)} %copy.12.groups_ref, s32[128,8]{1,0:T(8,128)} %copy.13.picks_ref, s32[128,8]{1,0:T(8,128)} %copy.14.gates_ref, s32[1]{0:T(128)S(6)} %copy.15.count_ref, ...), custom_call_target="tpu_custom_call" | custom-call | tf_op jit(solution)/shard_map/pallas_call | solution.py:277
  42.7 0.9 %reduce = f32[128]{0:T(128)S(1)} reduce(f32[128,1]{1,0:T(8,128)} %get-tuple-element.10, f32[]{:T(128)} %constant.1), dimensions={1}, to_apply=%get-tuple-element.10.reduce_sub_computation | reduce | bytes 1028 | tf_op jit(solution)/shard_map/pallas_call | solution.py:277
  43.6 2.8 %fusion = bf16[128,7168]{1,0:T(8,128)(2,1)} fusion(bf16[128,16]{1,0:T(8,128)(2,1)} %get-tuple-element.8, f32[128]{0:T(128)S(1)} %reduce, bf16[2,8,7168]{2,1,0:T(8,128)(2,1)} %get-tuple-element.9), kind=kOutput, calls=%fused_computation.1 | convolution fusion | flops 31195136 | bytes 2068992 | tf_op jit(solution)/shard_map/dot_general | solution.py:328

commit v2 on v1

v2 whole, which is shorter than its diff:
```python
import functools

import jax
import jax.numpy as jnp
from jax import lax
from jax.experimental import pallas as pl
from jax.experimental.pallas import tpu as pltpu
from jax.sharding import PartitionSpec as P

SPLIT = 8
GROUP_SIZE = 32
MESH = pl.DeviceIdType.MESH
SIB, NEAR, FAR = 1, 2, 4


def kernel(
    flight,
    cap,
    tokens_hbm,
    groups_ref,
    picks_ref,
    gates_ref,
    count_ref,
    gate_hbm,
    up_hbm,
    down_hbm,
    hit_ref,
    share_ref,
    outs_ref,
    tok,
    wgate,
    wup,
    wdown,
    send_unit,
    rows,
    part,
    part_bf,
    diag_in,
    sums_in,
    home_out,
    home_in,
    tok_sem,
    own_sem,
    wsend_sem,
    wrecv_sem,
    usend_sem,
    urecv_sem,
    nsend_sem,
    rrecv_sem,
    dsend_sem,
    drecv_sem,
    ssend_sem,
    srecv_sem,
    hsend_sem,
    hrecv_sem,
):
    me = lax.axis_index("node")
    group = me // SPLIT
    member = lax.rem(me, SPLIT)
    width = tok.shape[1]
    hid = gate_hbm.shape[1]
    token_rows = tok.shape[0]

    def flipped(bit):
        return me + bit - 2 * bit * lax.rem(me // bit, 2)

    sib, near, far = flipped(SIB), flipped(NEAR), flipped(FAR)

    def peer(step):
        return lax.rem(group + step, flight) * SPLIT + member

    tok_copy = pltpu.make_async_copy(tokens_hbm, tok, tok_sem)
    tok_copy.start()

    barrier = pltpu.get_barrier_semaphore()
    partners = [sib, near, far] + [peer(step) for step in range(1, flight)]
    for partner in partners:
        pl.semaphore_signal(barrier, inc=1, device_id={"node": partner}, device_id_type=MESH)

    mine, theirs = pl.ds(0, hid), pl.ds(hid, hid)
    own_copies = [
        pltpu.make_async_copy(gate_hbm, wgate.at[:, mine], own_sem.at[0]),
        pltpu.make_async_copy(up_hbm, wup.at[:, mine], own_sem.at[1]),
        pltpu.make_async_copy(down_hbm, wdown.at[mine, :], own_sem.at[2]),
    ]
    for copy in own_copies:
        copy.start()

    valid = lax.broadcasted_iota(jnp.int32, (1, token_rows), 1) < count_ref[0]
    gate_vals = gates_ref[...].astype(jnp.float32)
    weight = 2.5 * gate_vals / jnp.sum(gate_vals, axis=0, keepdims=True)
    picks = picks_ref[...]
    groups = groups_ref[...]
    place = lax.broadcasted_iota(jnp.int32, (flight * cap, token_rows), 0)
    picked = jnp.zeros((flight * cap, token_rows), jnp.float32)
    share = jnp.zeros((1, token_rows), jnp.float32)
    for step in range(flight):
        expert = lax.rem(group + step, flight)
        chosen = jnp.max((groups == expert).astype(jnp.float32), axis=0, keepdims=True)
        chosen = jnp.where(valid, chosen, 0.0)
        match = (picks == expert * GROUP_SIZE).astype(jnp.float32) * chosen
        share = share + jnp.sum(match * weight, axis=0, keepdims=True)
        here = jnp.max(match, axis=0, keepdims=True)
        in_step = (place >= step * cap) & (place < (step + 1) * cap)
        picked = jnp.where(in_step, here, picked)
    down_id = lax.broadcasted_iota(jnp.int32, (token_rows, token_rows), 0)
    right_id = lax.broadcasted_iota(jnp.int32, (token_rows, token_rows), 1)
    tri = (down_id <= right_id).astype(jnp.bfloat16)
    slot = jnp.dot(picked.astype(jnp.bfloat16), tri, preferred_element_type=jnp.float32) - 1.0
    want = lax.rem(place, cap).astype(jnp.float32)
    hit = jnp.where(slot == want, picked, 0.0).astype(jnp.bfloat16)
    hit_ref[...] = hit

    def remote(src, dst, send_sem, recv_sem, target):
        copy = pltpu.make_async_remote_copy(
            src_ref=src,
            dst_ref=dst,
            send_sem=send_sem,
            recv_sem=recv_sem,
            device_id={"node": target},
            device_id_type=MESH,
        )
        copy.start()
        return copy

    def arrived(dst, recv_sem):
        pltpu.make_async_copy(dst, dst, recv_sem).wait()

    pl.semaphore_wait(barrier, len(partners))
    w_copies = [
        remote(gate_hbm, wgate.at[:, theirs], wsend_sem.at[0], wrecv_sem.at[0], sib),
        remote(up_hbm, wup.at[:, theirs], wsend_sem.at[1], wrecv_sem.at[1], sib),
        remote(down_hbm, wdown.at[theirs, :], wsend_sem.at[2], wrecv_sem.at[2], sib),
    ]

    tok_copy.wait()
    chunk = width // 7 if width % (7 * 128) == 0 else width
    for at in range(0, width, chunk):
        cols = pl.ds(at, chunk)
        got = jnp.dot(hit, tok[:, cols], preferred_element_type=jnp.float32).astype(jnp.bfloat16)
        for step in range(flight):
            unit = got[step * cap : (step + 1) * cap]
            if step == 0:
                rows[0, 0, :, cols] = unit
            else:
                send_unit[step, :, cols] = unit

    cut = width // 128 * 3 // 4 * 128
    spans = (pl.ds(0, cut), pl.ds(cut, width - cut))
    LO, HI = 0, 1
    sent = []

    for step in range(1, flight):
        for half in (HI, LO):
            sent.append(
                remote(
                    send_unit.at[step, :, spans[half]],
                    rows.at[flight - step, 0, :, spans[half]],
                    usend_sem.at[step, half],
                    urecv_sem.at[flight - step, half],
                    peer(step),
                )
            )

    def pass_on(e, src, dst, half, target):
        number = 2 * (dst - 1) + half
        sent.append(
            remote(
                rows.at[e, src, :, spans[half]],
                rows.at[e, dst, :, spans[half]],
                nsend_sem.at[e, number],
                rrecv_sem.at[e, number],
                target,
            )
        )

    def got_rows(e, src, half):
        arrived(rows.at[e, src, :, spans[half]], rrecv_sem.at[e, 2 * (src - 1) + half])

    def spread(e, half):
        if half == HI:
            pass_on(e, 0, 1, half, near)
            pass_on(e, 0, 2, half, far)
        else:
            pass_on(e, 0, 2, half, far)
            pass_on(e, 0, 1, half, near)

    def forward(e):
        got_rows(e, 1, HI)
        pass_on(e, 1, 3, HI, far)
        got_rows(e, 2, LO)
        pass_on(e, 2, 3, LO, near)

    spread(0, HI)
    spread(0, LO)
    share_ref[...] = jnp.sum(jnp.where(down_id == right_id, share, 0.0), axis=1, keepdims=True)
    forward(0)
    for half in (HI, LO):
        for e in range(1, flight):
            arrived(rows.at[e, 0, :, spans[half]], urecv_sem.at[e, half])
            spread(e, half)

    def rest(e):
        got_rows(e, 1, LO)
        got_rows(e, 2, HI)
        got_rows(e, 3, HI)
        got_rows(e, 3, LO)

    def hidden(low, high):
        count = (high - low) * 4 * cap
        x = rows[low:high].reshape(count, width)
        gate_val = jnp.dot(x, wgate[...], preferred_element_type=jnp.float32)
        up_val = jnp.dot(x, wup[...], preferred_element_type=jnp.float32)
        return (gate_val / (1.0 + jnp.exp(-gate_val)) * up_val).astype(jnp.bfloat16)

    def project(h, low, high):
        for at in range(0, width, chunk):
            cols = pl.ds(at, chunk)
            val = jnp.dot(h, wdown[:, cols], preferred_element_type=jnp.float32)
            val = val.reshape(high - low, 4, cap, chunk)
            part[low:high, :, :, cols] = val
            part_bf[low:high, :, :, cols] = val.astype(jnp.bfloat16)

    def send_diag(e, half):
        sent.append(
            remote(
                part_bf.at[e, 3, :, spans[half]],
                diag_in.at[e, :, spans[half]],
                dsend_sem.at[e, half],
                drecv_sem.at[e, half],
                near if half == LO else far,
            )
        )

    def send_sum(e, way, half):
        number = 2 * way + half
        sent.append(
            remote(
                part_bf.at[e, 1 + way, :, spans[half]],
                sums_in.at[e, way, :, spans[half]],
                ssend_sem.at[e, number],
                srecv_sem.at[e, number],
                far if way else near,
            )
        )

    def give_back(e):
        send_diag(e, HI)
        send_diag(e, LO)
        send_sum(e, 1, HI)
        send_sum(e, 0, LO)

    rest(0)
    for number in range(2):
        own_copies[number].wait()
        w_copies[number].wait_recv()
    hidden_first = hidden(0, 1)
    for e in range(1, flight):
        forward(e)
    own_copies[2].wait()
    w_copies[2].wait_recv()
    project(hidden_first, 0, 1)
    give_back(0)
    if flight > 1:
        for e in range(1, flight):
            rest(e)
        project(hidden(1, flight), 1, flight)
        for e in range(1, flight):
            give_back(e)

    for e in range(flight):
        for half, way in ((HI, 0), (LO, 1)):
            cols = spans[half]
            arrived(diag_in.at[e, :, cols], drecv_sem.at[e, half])
            val = part[e, 1 + way, :, cols] + diag_in[e, :, cols].astype(jnp.float32)
            part_bf[e, 1 + way, :, cols] = val.astype(jnp.bfloat16)
            send_sum(e, way, half)

    def total(e, half):
        cols = spans[half]
        for way in range(2):
            arrived(sums_in.at[e, way, :, cols], srecv_sem.at[e, 2 * way + half])
        val = part[e, 0, :, cols] + sums_in[e, 0, :, cols].astype(jnp.float32)
        val = val + sums_in[e, 1, :, cols].astype(jnp.float32)
        return val.astype(jnp.bfloat16)

    for e in range(1, flight):
        for half in (HI, LO):
            cols = spans[half]
            home_out[e, :, cols] = total(e, half)
            sent.append(
                remote(
                    home_out.at[e, :, cols],
                    home_in.at[flight - e, :, cols],
                    hsend_sem.at[e, half],
                    hrecv_sem.at[flight - e, half],
                    peer(e),
                )
            )
    for half in (HI, LO):
        outs_ref[0, :, spans[half]] = total(0, half)
    for step in range(1, flight):
        for half in (HI, LO):
            arrived(home_in.at[step, :, spans[half]], hrecv_sem.at[step, half])
        outs_ref[step] = home_in[step]

    for copy in sent + w_copies:
        copy.wait_send()


def combine(hit_ref, share_ref, outs_ref, routed_ref):
    back = lax.dot_general(
        hit_ref[...], outs_ref[...], (((0,), (0,)), ((), ())), preferred_element_type=jnp.float32
    )
    routed_ref[...] = (back * share_ref[...]).astype(routed_ref.dtype)


def local(
    tokens,
    group_choice,
    expert_picks,
    gate_fixed,
    token_counts,
    expert_gate,
    expert_up,
    expert_down,
):
    flight = lax.axis_size("node") // SPLIT
    token_rows, width = tokens.shape
    cap = token_rows // 16
    hid = expert_gate.shape[1]
    vmem = pl.BlockSpec(memory_space=pltpu.VMEM)
    anywhere = pl.BlockSpec(memory_space=pl.ANY)
    dma = pltpu.SemaphoreType.DMA
    hit, share, outs = pl.pallas_call(
        functools.partial(kernel, flight, cap),
        out_shape=(
            jax.ShapeDtypeStruct((flight * cap, token_rows), jnp.bfloat16),
            jax.ShapeDtypeStruct((token_rows, 1), jnp.float32),
            jax.ShapeDtypeStruct((flight, cap, width), jnp.bfloat16),
        ),
        in_specs=[
            anywhere,
            vmem,
            vmem,
            vmem,
            pl.BlockSpec(memory_space=pltpu.SMEM),
            anywhere,
            anywhere,
            anywhere,
        ],
        out_specs=(vmem, vmem, vmem),
        scratch_shapes=[
            pltpu.VMEM((token_rows, width), jnp.bfloat16),
            pltpu.VMEM((width, 2 * hid), jnp.bfloat16),
            pltpu.VMEM((width, 2 * hid), jnp.bfloat16),
            pltpu.VMEM((2 * hid, width), jnp.bfloat16),
            pltpu.VMEM((flight, cap, width), jnp.bfloat16),
            pltpu.VMEM((flight, 4, cap, width), jnp.bfloat16),
            pltpu.VMEM((flight, 4, cap, width), jnp.float32),
            pltpu.VMEM((flight, 4, cap, width), jnp.bfloat16),
            pltpu.VMEM((flight, cap, width), jnp.bfloat16),
            pltpu.VMEM((flight, 2, cap, width), jnp.bfloat16),
            pltpu.VMEM((flight, cap, width), jnp.bfloat16),
            pltpu.VMEM((flight, cap, width), jnp.bfloat16),
            dma(()),
            dma((3,)),
            dma((3,)),
            dma((3,)),
            dma((flight, 2)),
            dma((flight, 2)),
            dma((flight, 6)),
            dma((flight, 6)),
            dma((flight, 2)),
            dma((flight, 2)),
            dma((flight, 4)),
            dma((flight, 4)),
            dma((flight, 2)),
            dma((flight, 2)),
        ],
        compiler_params=pltpu.CompilerParams(
            collective_id=0, has_side_effects=True, vmem_limit_bytes=56 * 1024 * 1024
        ),
    )(tokens, group_choice.T, expert_picks.T, gate_fixed.T, token_counts, expert_gate, expert_up, expert_down)
    block = width // 4 if width % 512 == 0 else width
    return pl.pallas_call(
        combine,
        grid=(width // block,),
        out_shape=jax.ShapeDtypeStruct((token_rows, width), tokens.dtype),
        in_specs=[
            pl.BlockSpec((flight * cap, token_rows), lambda i: (0, 0)),
            pl.BlockSpec((token_rows, 1), lambda i: (0, 0)),
            pl.BlockSpec((flight * cap, block), lambda i: (0, i)),
        ],
        out_specs=pl.BlockSpec((token_rows, block), lambda i: (0, i)),
    )(hit, share, outs.reshape(flight * cap, width))


def solution(mesh):
    return jax.shard_map(
        local,
        mesh=mesh,
        in_specs=(
            P(("rep", "node"), None),
            P(("rep", "node"), None),
            P(("rep", "node"), None),
            P(("rep", "node"), None),
            P(("rep", "node")),
            P(None, "node"),
            P(None, "node"),
            P("node", None),
        ),
        out_specs=P(("rep", "node"), None),
        check_vma=False,
    )
```

time: 47.1 us -> 41.1 us (0.87)
  local copies, waits for them, and re-layouts: 4.24 us -> 0 us
  matrix products: 2.81 us -> 0 us
  Pallas kernels: 37.8 us -> 40.1 us
  other arithmetic: 0.94 us -> 0 us
    unnamed x3 -> x0, local copies, waits for them, and re-layouts: 4.24 us -> none
    pallas_call x0 -> x1, Pallas kernels: none -> 3.88 us  [local(): pl.pallas_call(combine, grid=(width // block,), out_shape=jax.ShapeDtypeS...]
    dot_general x1 -> x0, matrix products: 2.81 us -> none  [local(): jnp.dot(hit, outs.reshape(flight * cap, width), preferred_element_type=jn...]
    pallas_call x1, Pallas kernels: 37.8 us -> 36.2 us  [local(): pl.pallas_call(functools.partial(kernel, flight, cap), out_shape=(jax.Sha...]
    pallas_call x1 -> x0, other arithmetic: 0.94 us -> none  [local(): pl.pallas_call(functools.partial(kernel, flight, cap), out_shape=(jax.Sha...]
where the time goes in v2:
time: 41.1 us; the launch traced here: 40.8 us
  Pallas kernels  40.1 us (98%)
  between operations  0.66 us (2%)
    pallas_call x1, Pallas kernels, local(): pl.pallas_call(functools.partial(kernel, flight, cap), out_shape=(jax.Sha...  36.2 us
    pallas_call x1, Pallas kernels, local(): pl.pallas_call(combine, grid=(width // block,), out_shape=jax.ShapeDtypeS...  3.88 us

profile of v2, /device:TPU:0, one launch (start us, length us, event | category | flops | bytes accessed | tf_op | source)
XLA Modules:
  0.0 40.8 jit_solution(10031739149864167320)
XLA Ops:
  0.7 36.2 %shard_map.82 = (bf16[16,128]{1,0:T(8,128)(2,1)}, f32[128,1]{1,0:T(8,128)}, bf16[2,8,7168]{2,1,0:T(8,128)(2,1)}) custom-call(bf16[128,7168]{1,0:T(8,128)(2,1)} %tokens_hbm.1, s32[4,128]{1,0:T(4,128)} %bitcast.7, s32[8,128]{1,0:T(8,128)} %bitcast.5, s32[8,128]{1,0:T(8,128)} %bitcast.6, s32[1]{0:T(128)S(6)} %copy.9.count_ref, bf16[7168,128]{1,0:T(8,128)(2,1)} %gate_hbm.1, ...), custom_call_target="tpu_custom_call" | custom-call | tf_op jit(solution)/shard_map/pallas_call | solution.py:335
  36.9 3.9 %shard_map.83 = bf16[128,7168]{1,0:T(8,128)(2,1)} custom-call(bf16[16,128]{1,0:T(8,128)(2,1)} %get-tuple-element.8.hit_ref, f32[128,1]{1,0:T(8,128)} %get-tuple-element.9.share_ref, bf16[16,7168]{1,0:T(8,128)(2,1)} %bitcast.4), custom_call_target="tpu_custom_call" | custom-call | tf_op jit(solution)/shard_map/pallas_call | solution.py:386

commit v3 on v2

--- a/solution.py
+++ b/solution.py
@@ -83,9 +83,6 @@
         pltpu.make_async_copy(up_hbm, wup.at[:, mine], own_sem.at[1]),
         pltpu.make_async_copy(down_hbm, wdown.at[mine, :], own_sem.at[2]),
     ]
-    for copy in own_copies:
-        copy.start()
-
     valid = lax.broadcasted_iota(jnp.int32, (1, token_rows), 1) < count_ref[0]
     gate_vals = gates_ref[...].astype(jnp.float32)
     weight = 2.5 * gate_vals / jnp.sum(gate_vals, axis=0, keepdims=True)
@@ -110,6 +107,7 @@
     want = lax.rem(place, cap).astype(jnp.float32)
     hit = jnp.where(slot == want, picked, 0.0).astype(jnp.bfloat16)
     hit_ref[...] = hit
+    share_ref[...] = share
 
     def remote(src, dst, send_sem, recv_sem, target):
         copy = pltpu.make_async_remote_copy(
@@ -127,31 +125,14 @@
         pltpu.make_async_copy(dst, dst, recv_sem).wait()
 
     pl.semaphore_wait(barrier, len(partners))
-    w_copies = [
-        remote(gate_hbm, wgate.at[:, theirs], wsend_sem.at[0], wrecv_sem.at[0], sib),
-        remote(up_hbm, wup.at[:, theirs], wsend_sem.at[1], wrecv_sem.at[1], sib),
-        remote(down_hbm, wdown.at[theirs, :], wsend_sem.at[2], wrecv_sem.at[2], sib),
-    ]
-
-    tok_copy.wait()
-    chunk = width // 7 if width % (7 * 128) == 0 else width
-    for at in range(0, width, chunk):
-        cols = pl.ds(at, chunk)
-        got = jnp.dot(hit, tok[:, cols], preferred_element_type=jnp.float32).astype(jnp.bfloat16)
-        for step in range(flight):
-            unit = got[step * cap : (step + 1) * cap]
-            if step == 0:
-                rows[0, 0, :, cols] = unit
-            else:
-                send_unit[step, :, cols] = unit
 
     cut = width // 128 * 3 // 4 * 128
     spans = (pl.ds(0, cut), pl.ds(cut, width - cut))
     LO, HI = 0, 1
     sent = []
 
-    for step in range(1, flight):
-        for half in (HI, LO):
+    def send_units(half):
+        for step in range(1, flight):
             sent.append(
                 remote(
                     send_unit.at[step, :, spans[half]],
@@ -191,9 +172,30 @@
         got_rows(e, 2, LO)
         pass_on(e, 2, 3, LO, near)
 
-    spread(0, HI)
-    spread(0, LO)
-    share_ref[...] = jnp.sum(jnp.where(down_id == right_id, share, 0.0), axis=1, keepdims=True)
+    def pieces(half):
+        low, high = (0, cut) if half == LO else (cut, width)
+        step = 6 * 128
+        return [pl.ds(at, min(step, high - at)) for at in range(low, high, step)]
+
+    tok_copy.wait()
+    for half in (HI, LO):
+        for cols in pieces(half):
+            got = jnp.dot(hit, tok[:, cols], preferred_element_type=jnp.float32).astype(jnp.bfloat16)
+            for step in range(flight):
+                unit = got[step * cap : (step + 1) * cap]
+                if step == 0:
+                    rows[0, 0, :, cols] = unit
+                else:
+                    send_unit[step, :, cols] = unit
+        send_units(half)
+        spread(0, half)
+    for copy in own_copies:
+        copy.start()
+    w_copies = [
+        remote(gate_hbm, wgate.at[:, theirs], wsend_sem.at[0], wrecv_sem.at[0], sib),
+        remote(up_hbm, wup.at[:, theirs], wsend_sem.at[1], wrecv_sem.at[1], sib),
+        remote(down_hbm, wdown.at[theirs, :], wsend_sem.at[2], wrecv_sem.at[2], sib),
+    ]
     forward(0)
     for half in (HI, LO):
         for e in range(1, flight):
@@ -212,14 +214,6 @@
         gate_val = jnp.dot(x, wgate[...], preferred_element_type=jnp.float32)
         up_val = jnp.dot(x, wup[...], preferred_element_type=jnp.float32)
         return (gate_val / (1.0 + jnp.exp(-gate_val)) * up_val).astype(jnp.bfloat16)
-
-    def project(h, low, high):
-        for at in range(0, width, chunk):
-            cols = pl.ds(at, chunk)
-            val = jnp.dot(h, wdown[:, cols], preferred_element_type=jnp.float32)
-            val = val.reshape(high - low, 4, cap, chunk)
-            part[low:high, :, :, cols] = val
-            part_bf[low:high, :, :, cols] = val.astype(jnp.bfloat16)
 
     def send_diag(e, half):
         sent.append(
@@ -244,11 +238,16 @@
             )
         )
 
-    def give_back(e):
-        send_diag(e, HI)
-        send_diag(e, LO)
-        send_sum(e, 1, HI)
-        send_sum(e, 0, LO)
+    def project(h, low, high):
+        for half in (LO, HI):
+            for cols in pieces(half):
+                val = jnp.dot(h, wdown[:, cols], preferred_element_type=jnp.float32)
+                val = val.reshape(high - low, 4, cap, cols.size)
+                part[low:high, :, :, cols] = val
+                part_bf[low:high, :, :, cols] = val.astype(jnp.bfloat16)
+            for e in range(low, high):
+                send_diag(e, half)
+                send_sum(e, 0 if half == LO else 1, half)
 
     rest(0)
     for number in range(2):
@@ -260,13 +259,10 @@
     own_copies[2].wait()
     w_copies[2].wait_recv()
     project(hidden_first, 0, 1)
-    give_back(0)
     if flight > 1:
         for e in range(1, flight):
             rest(e)
         project(hidden(1, flight), 1, flight)
-        for e in range(1, flight):
-            give_back(e)
 
     for e in range(flight):
         for half, way in ((HI, 0), (LO, 1)):
@@ -306,13 +302,6 @@
 
     for copy in sent + w_copies:
         copy.wait_send()
-
-
-def combine(hit_ref, share_ref, outs_ref, routed_ref):
-    back = lax.dot_general(
-        hit_ref[...], outs_ref[...], (((0,), (0,)), ((), ())), preferred_element_type=jnp.float32
-    )
-    routed_ref[...] = (back * share_ref[...]).astype(routed_ref.dtype)
 
 
 def local(
@@ -336,7 +325,7 @@
         functools.partial(kernel, flight, cap),
         out_shape=(
             jax.ShapeDtypeStruct((flight * cap, token_rows), jnp.bfloat16),
-            jax.ShapeDtypeStruct((token_rows, 1), jnp.float32),
+            jax.ShapeDtypeStruct((1, token_rows), jnp.float32),
             jax.ShapeDtypeStruct((flight, cap, width), jnp.bfloat16),
         ),
         in_specs=[
@@ -382,18 +371,13 @@
             collective_id=0, has_side_effects=True, vmem_limit_bytes=56 * 1024 * 1024
         ),
     )(tokens, group_choice.T, expert_picks.T, gate_fixed.T, token_counts, expert_gate, expert_up, expert_down)
-    block = width // 4 if width % 512 == 0 else width
-    return pl.pallas_call(
-        combine,
-        grid=(width // block,),
-        out_shape=jax.ShapeDtypeStruct((token_rows, width), tokens.dtype),
-        in_specs=[
-            pl.BlockSpec((flight * cap, token_rows), lambda i: (0, 0)),
-            pl.BlockSpec((token_rows, 1), lambda i: (0, 0)),
-            pl.BlockSpec((flight * cap, block), lambda i: (0, i)),
-        ],
-        out_specs=pl.BlockSpec((token_rows, block), lambda i: (0, i)),
-    )(hit, share, outs.reshape(flight * cap, width))
+    back = lax.dot_general(
+        hit,
+        outs.reshape(flight * cap, width),
+        (((0,), (0,)), ((), ())),
+        preferred_element_type=jnp.float32,
+    )
+    return (back * share.reshape(token_rows)[:, None]).astype(tokens.dtype)
 
 
 def solution(mesh):

time: 41.1 us -> 41.3 us (level)
  matrix products: 0 us -> 2.83 us
  Pallas kernels: 40.1 us -> 37.6 us
    pallas_call x1 -> x0, Pallas kernels: 3.88 us -> none  [local(): pl.pallas_call(combine, grid=(width // block,), out_shape=jax.ShapeDtypeS...]
    dot_general x0 -> x1, matrix products: none -> 2.83 us  [local(): lax.dot_general(hit, outs.reshape(flight * cap, width), (((0,), (0,)), ((...]
    pallas_call x1, Pallas kernels: 36.2 us -> 37.6 us  [local(): pl.pallas_call(functools.partial(kernel, flight, cap), out_shape=(jax.Sha...]
where the time goes in v3:
time: 41.3 us; the launch traced here: 41.1 us
  Pallas kernels  37.6 us (91%)
  matrix products  2.83 us (7%)
  between operations  0.66 us (2%)
    pallas_call x1, Pallas kernels, local(): pl.pallas_call(functools.partial(kernel, flight, cap), out_shape=(jax.Sha...  37.6 us
    dot_general x1, matrix products, local(): lax.dot_general(hit, outs.reshape(flight * cap, width), (((0,), (0,)), ((...  2.83 us

profile of v3, /device:TPU:0, one launch (start us, length us, event | category | flops | bytes accessed | tf_op | source)
XLA Modules:
  0.0 41.1 jit_solution(7828870273048792857)
XLA Ops:
  0.7 37.6 %shard_map.82 = (bf16[16,128]{1,0:T(8,128)(2,1)}, f32[1,128]{1,0:T(1,128)}, bf16[2,8,7168]{2,1,0:T(8,128)(2,1)}) custom-call(bf16[128,7168]{1,0:T(8,128)(2,1)} %tokens_hbm.1, s32[4,128]{1,0:T(4,128)} %bitcast.10, s32[8,128]{1,0:T(8,128)} %bitcast.8, s32[8,128]{1,0:T(8,128)} %bitcast.9, s32[1]{0:T(128)S(6)} %copy.9.count_ref, bf16[7168,128]{1,0:T(8,128)(2,1)} %gate_hbm.1, ...), custom_call_target="tpu_custom_call" | custom-call | tf_op jit(solution)/shard_map/pallas_call | solution.py:324
  38.3 2.8 %fusion = bf16[128,7168]{1,0:T(8,128)(2,1)} fusion(bf16[16,128]{1,0:T(8,128)(2,1)} %get-tuple-element.8, f32[128]{0:T(128)} %bitcast.11, bf16[2,8,7168]{2,1,0:T(8,128)(2,1)} %get-tuple-element.9), kind=kOutput, calls=%fused_computation.1 | convolution fusion | flops 31195136 | bytes 2068992 | tf_op jit(solution)/shard_map/dot_general | solution.py:374

commit v4 on v3

--- a/solution.py
+++ b/solution.py
@@ -83,6 +83,9 @@
         pltpu.make_async_copy(up_hbm, wup.at[:, mine], own_sem.at[1]),
         pltpu.make_async_copy(down_hbm, wdown.at[mine, :], own_sem.at[2]),
     ]
+    for copy in own_copies:
+        copy.start()
+
     valid = lax.broadcasted_iota(jnp.int32, (1, token_rows), 1) < count_ref[0]
     gate_vals = gates_ref[...].astype(jnp.float32)
     weight = 2.5 * gate_vals / jnp.sum(gate_vals, axis=0, keepdims=True)
@@ -125,6 +128,11 @@
         pltpu.make_async_copy(dst, dst, recv_sem).wait()
 
     pl.semaphore_wait(barrier, len(partners))
+    w_copies = [
+        remote(gate_hbm, wgate.at[:, theirs], wsend_sem.at[0], wrecv_sem.at[0], sib),
+        remote(up_hbm, wup.at[:, theirs], wsend_sem.at[1], wrecv_sem.at[1], sib),
+        remote(down_hbm, wdown.at[theirs, :], wsend_sem.at[2], wrecv_sem.at[2], sib),
+    ]
 
     cut = width // 128 * 3 // 4 * 128
     spans = (pl.ds(0, cut), pl.ds(cut, width - cut))
@@ -189,13 +197,6 @@
                     send_unit[step, :, cols] = unit
         send_units(half)
         spread(0, half)
-    for copy in own_copies:
-        copy.start()
-    w_copies = [
-        remote(gate_hbm, wgate.at[:, theirs], wsend_sem.at[0], wrecv_sem.at[0], sib),
-        remote(up_hbm, wup.at[:, theirs], wsend_sem.at[1], wrecv_sem.at[1], sib),
-        remote(down_hbm, wdown.at[theirs, :], wsend_sem.at[2], wrecv_sem.at[2], sib),
-    ]
     forward(0)
     for half in (HI, LO):
         for e in range(1, flight):

time: 41.3 us -> 41.3 us (level)
  no operation moved by 1% of the time
where the time goes in v4:
time: 41.3 us; the launch traced here: 41.1 us
  Pallas kernels  37.6 us (91%)
  matrix products  2.83 us (7%)
  between operations  0.66 us (2%)
    pallas_call x1, Pallas kernels, local(): pl.pallas_call(functools.partial(kernel, flight, cap), out_shape=(jax.Sha...  37.6 us
    dot_general x1, matrix products, local(): lax.dot_general(hit, outs.reshape(flight * cap, width), (((0,), (0,)), ((...  2.83 us

profile of v4, /device:TPU:0, one launch (start us, length us, event | category | flops | bytes accessed | tf_op | source)
XLA Modules:
  0.0 41.1 jit_solution(15966968878561406491)
XLA Ops:
  0.7 37.6 %shard_map.82 = (bf16[16,128]{1,0:T(8,128)(2,1)}, f32[1,128]{1,0:T(1,128)}, bf16[2,8,7168]{2,1,0:T(8,128)(2,1)}) custom-call(bf16[128,7168]{1,0:T(8,128)(2,1)} %tokens_hbm.1, s32[4,128]{1,0:T(4,128)} %bitcast.10, s32[8,128]{1,0:T(8,128)} %bitcast.8, s32[8,128]{1,0:T(8,128)} %bitcast.9, s32[1]{0:T(128)S(6)} %copy.9.count_ref, bf16[7168,128]{1,0:T(8,128)(2,1)} %gate_hbm.1, ...), custom_call_target="tpu_custom_call" | custom-call | tf_op jit(solution)/shard_map/pallas_call | solution.py:325
  38.3 2.8 %fusion = bf16[128,7168]{1,0:T(8,128)(2,1)} fusion(bf16[16,128]{1,0:T(8,128)(2,1)} %get-tuple-element.8, f32[128]{0:T(128)} %bitcast.11, bf16[2,8,7168]{2,1,0:T(8,128)(2,1)} %get-tuple-element.9), kind=kOutput, calls=%fused_computation.1 | convolution fusion | flops 31195136 | bytes 2068992 | tf_op jit(solution)/shard_map/dot_general | solution.py:375
